TPU v7x, 32 devices: a whole 2x2x4 slice. The times are simulated.
32 devices in a mesh: layers: 2 (over x), row: 16 (over z, y, core).
Axes of the slice: x: 2, y: 2, z: 4, core: 2. Of those that a mesh axis runs over, the one named last changes fastest.
Arguments:
- iterate: bfloat16 [10240, 4096], P(('layers', 'row')), parts along dimension 0, may hold values from -0.0390625 to 0.0390625
Outputs:
- update: bfloat16 [10240, 4096], P(('layers', 'row')), parts along dimension 0
There are 2 independent parts, one for each index of `layers`. A program takes and returns all parts, laid end to end along the dimension named above; each array names one. Nothing has to cross between parts.
All inputs are finite; a program needn't handle non-finite values.
Results may differ from a plain program's by a relative error of at most 0.0057.
Values may be sent and summed in bfloat16 or wider, within the bound.
A program may use at most 128 MiB of HBM per device.

v0:
```python
import math

import jax
import jax.numpy as jnp
from jax import lax
from jax.sharding import PartitionSpec as P


def body(iterate):
    rows = iterate.shape[0]
    width = iterate.shape[1]
    count = lax.axis_size("row")
    total_rows = rows * count
    whole = lax.all_gather(iterate, "row", axis=0, tiled=True)
    gram = lax.dot_general(
        iterate, whole, (((1,), (1,)), ((), ())), preferred_element_type=jnp.float32
    ).astype(jnp.bfloat16)
    carried = jnp.dot(gram, whole, preferred_element_type=jnp.float32).astype(jnp.bfloat16)
    square = lax.dot_general(
        carried, whole, (((1,), (1,)), ((), ())), preferred_element_type=jnp.float32
    )
    poly = (-4.775 * gram.astype(jnp.float32) + 2.0315 * square).astype(jnp.bfloat16)
    after = 3.4445 * iterate.astype(jnp.float32) + jnp.dot(
        poly, whole, preferred_element_type=jnp.float32
    )
    return (after * math.sqrt(max(total_rows, width))).astype(jnp.bfloat16)


def solution(mesh):
    in_specs = (P(("layers", "row"), None),)
    out_specs = P(("layers", "row"), None)
    return jax.shard_map(body, mesh=mesh, in_specs=in_specs, out_specs=out_specs, check_vma=False)
```

profile of v0, /device:TPU:0, one launch (start us, length us, event | category | flops | bytes accessed | tf_op | source)
XLA Modules:
  0.0 312.8 jit_solution(12075295816072033307)
XLA Ops:
  6.5 0.0 all-gather.2.cloned.1.call-start
  6.5 0.7 all-gather.2.cloned.1.call-update
  7.3 212.0 %all-gather.2.cloned.1.call-done = bf16[5120,4096]{1,0:T(8,128)(2,1)} async-done(((bf16[320,4096]{1,0:T(8,128)(2,1)}), bf16[5120,4096]{1,0:T(8,128)(2,1)}) %all-gather.2.cloned.1.call-update) | async-done | bytes 41943056 | tf_op jit(solution)/shard_map/all_gather | solution.py:14
  219.3 19.6 %convolution_convert_fusion = bf16[320,5120]{1,0:T(8,128)(2,1)S(1)} fusion(bf16[320,4096]{1,0:T(8,128)(2,1)} %param.1, bf16[5120,4096]{1,0:T(8,128)(2,1)} %all-gather.2.cloned.1.call-done), kind=kOutput, calls=%fused_computation.3 | convolution fusion | flops 13423411200 | bytes 47841280 | tf_op jit(solution)/shard_map/dot_general | solution.py:15
  238.9 0.0 copy-start.1
  238.9 1.7 copy-done.1
  240.6 20.7 %convolution_convert_fusion.1 = bf16[320,4096]{1,0:T(8,128)(2,1)} fusion(bf16[320,5120]{1,0:T(8,128)(2,1)S(1)} %convolution_convert_fusion, bf16[5120,4096]{1,0:T(8,128)(2,1)} %all-gather.2.cloned.1.call-done), kind=kOutput, calls=%fused_computation.6 | convolution fusion | flops 13423083520 | bytes 47841280 | tf_op jit(solution)/shard_map/dot_general | solution.py:18
  261.3 0.0 copy-start
  261.3 21.6 %fusion.1.clone.6 = bf16[320,5120]{1,0:T(8,128)(2,1)} fusion(bf16[320,4096]{1,0:T(8,128)(2,1)} %convolution_convert_fusion.1, bf16[5120,4096]{1,0:T(8,128)(2,1)} %all-gather.2.cloned.1.call-done, bf16[320,5120]{1,0:T(8,128)(2,1)} %copy-done.1), kind=kOutput, calls=%fused_computation.2.clone.clone.clone.clone.clone.1 | convolution fusion | flops 13429964800 | bytes 51118080 | tf_op jit(solution)/shard_map/dot_general | solution.py:19
  282.8 0.0 copy-done
  282.8 23.1 %fusion.3 = bf16[320,4096]{1,0:T(8,128)(2,1)} fusion(bf16[5120,4096]{1,0:T(8,128)(2,1)} %all-gather.2.cloned.1.call-done, bf16[320,4096]{1,0:T(8,128)(2,1)S(1)} %copy-done, bf16[320,5120]{1,0:T(8,128)(2,1)} %fusion.1.clone.6), kind=kOutput, calls=%fused_computation.7 | convolution fusion | flops 13428326400 | bytes 50462720 | tf_op jit(solution)/shard_map/dot_general | solution.py:23
Async XLA Ops:
  6.5 212.7 %all-gather.2.cloned.1.call-start = ((), (), s32[]{:S(2)}) async-start(), calls=%async_computation | async-start | bytes 44564480 | tf_op jit(solution)/shard_map/all_gather | solution.py:14
  238.9 1.8 copy-start.1
  261.3 21.6 %copy-start = (bf16[320,4096]{1,0:T(8,128)(2,1)S(1)}, bf16[320,4096]{1,0:T(8,128)(2,1)}, u32[]{:S(2)}) copy-start(bf16[320,4096]{1,0:T(8,128)(2,1)} %param.1) | copy-start | bytes 7864324
Sparse Core Ops, SparseCore 0:
  9.0 210.2 all-gather.1
where the time goes:
time: 313 us
  waiting for transfers between devices  213 us (68%)
  matrix products  84.9 us (27%)
  between operations  13.4 us (4%)
    all_gather x1, waiting for transfers between devices, body(): whole = lax.all_gather(iterate, 'row', axis=0, tiled=True)  212 us
    dot_general x1, matrix products, body(): jnp.dot(poly, whole, preferred_element_type=jnp.float32)  23.1 us
    dot_general x1, matrix products, body(): lax.dot_general(carried, whole, (((1,), (1,)), ((), ())), preferred_eleme...  21.6 us
    dot_general x1, matrix products, body(): jnp.dot(gram, whole, preferred_element_type=jnp.float32)  20.7 us
    dot_general x1, matrix products, body(): lax.dot_general(iterate, whole, (((1,), (1,)), ((), ())), preferred_eleme...  19.6 us
  transfers between devices with their start and end apart: 1, of which 1 were waited for; matrix products, arithmetic and copies ran while one was open for 0% of the time, Pallas kernels for 0%

commit v1 on v0

v1 whole, which is shorter than its diff:
```python
import functools
import math

import jax
import jax.numpy as jnp
from jax import lax
from jax.experimental import pallas as pl
from jax.experimental.pallas import tpu as pltpu
from jax.sharding import PartitionSpec as P

WIDE = 512
HOP = 1
AHEAD = 3
MESH = pl.DeviceIdType.MESH
NT = (((1,), (1,)), ((), ()))
TN = (((0,), (0,)), ((), ()))


def kernel(planes, x_ref, o_ref, quad, s, part, ups, downs, acc, mid, *sems):
    (xy_s, xy_r, xc_s, xc_r, xf_s, xf_r, u_s, u_r, d_s, d_r, gy_s, gy_r, gc_s, gc_r, gf_s, gf_r) = sems
    rows, width = x_ref.shape
    chunks = width // WIDE
    steps = part.shape[0]
    layer = lax.axis_index("layers")
    me = lax.axis_index("row")
    z = me // 4
    q = me % 4
    q_core = q + 1 - 2 * (q % 2)
    q_y = (q + 2) % 4
    core = me - q + q_core
    mate = me - q + q_y
    count = 4 * planes
    above = (me + 4) % count
    below = (me + count - 4) % count

    def remote(src, dst, send, recv, to):
        return pltpu.make_async_remote_copy(
            src_ref=src, dst_ref=dst, send_sem=send, recv_sem=recv, device_id=(layer, to), device_id_type=MESH
        )

    def at(t):
        return pl.ds(pl.multiple_of(t * WIDE, WIDE), WIDE)

    def of(member):
        return pl.ds(pl.multiple_of(member * rows, 16), rows)

    def send_y(t):
        return remote(x_ref.at[:, at(t)], quad.at[of(q), at(t)], xy_s.at[t], xy_r.at[t], mate)

    def send_core(t):
        return remote(x_ref.at[:, at(t)], quad.at[of(q), at(t)], xc_s.at[t], xc_r.at[t], core)

    def pass_core(t):
        piece = quad.at[of(q_y), at(t)]
        return remote(piece, piece, xf_s.at[t], xf_r.at[t], core)

    def send_up(k):
        return remote(ups.at[k], ups.at[k], u_s.at[k], u_r.at[k], above)

    def send_down(k):
        return remote(downs.at[k], downs.at[k], d_s.at[k], d_r.at[k], below)

    def sum_y(k):
        return remote(s.at[4 * k + q], s.at[4 * k + q], gy_s.at[k], gy_r.at[k], mate)

    def sum_core(k):
        return remote(s.at[4 * k + q], s.at[4 * k + q], gc_s.at[k], gc_r.at[k], core)

    def sum_pass(k):
        return remote(s.at[4 * k + q_y], s.at[4 * k + q_y], gf_s.at[k], gf_r.at[k], core)

    def where(b):
        t = 0
        for c in range(1, chunks):
            t = t + (b + 1024 - c * (c + 1) // 2) // 1024
        return b - t * (t + 1) // 2, t

    barrier = pltpu.get_barrier_semaphore()
    for other in (core, mate, above, below):
        pl.semaphore_signal(barrier, inc=1, device_id=(layer, other), device_id_type=MESH)
    pl.semaphore_wait(barrier, 4)

    for t in range(min(AHEAD, chunks)):
        send_y(t).start()
    for t in range(chunks):
        send_core(t).start()
    quad[of(q), :] = x_ref[...]
    acc[...] = jnp.zeros_like(acc)

    def chunk(t):
        send_y(t).wait_recv()
        pass_core(t).start()
        send_y(t).wait_send()

        @pl.when(t + AHEAD < chunks)
        def _():
            send_y(t + AHEAD).start()

        send_core(t).wait_recv()
        pass_core(t).wait_recv()

    def multiply(b, into, left):
        j, t = where(b)
        into[:, at(t)] += jnp.dot(left[:, at(j)], s[b], preferred_element_type=jnp.float32)

        @pl.when(j < t)
        def _():
            into[:, at(j)] += lax.dot_general(left[:, at(t)], s[b], NT, preferred_element_type=jnp.float32)

    chunk(0)
    chunk(1)
    delay = HOP * (planes - 1)

    def step(i, carry):
        @pl.when(i + 2 < chunks)
        def _():
            chunk(i + 2)

        @pl.when(i < steps)
        def _():
            j, t = where(4 * i + q)
            part[i] = lax.dot_general(
                quad[:, at(j)], quad[:, at(t)], TN, preferred_element_type=jnp.float32
            ).astype(jnp.bfloat16)

        k = i - HOP * z

        @pl.when((k >= 0) & (k < steps))
        def _():
            @pl.when(z == 0)
            def _():
                ups[k] = part[k]

            @pl.when(z > 0)
            def _():
                send_up(k).wait_recv()
                ups[k] = (ups[k].astype(jnp.float32) + part[k].astype(jnp.float32)).astype(jnp.bfloat16)

            @pl.when(z < planes - 1)
            def _():
                send_up(k).start()

        n = i - HOP * (planes - 1 - z)

        @pl.when((n >= 0) & (n < steps))
        def _():
            @pl.when(z == planes - 1)
            def _():
                downs[n] = part[n]

            @pl.when(z < planes - 1)
            def _():
                send_down(n).wait_recv()
                downs[n] = (downs[n].astype(jnp.float32) + part[n].astype(jnp.float32)).astype(jnp.bfloat16)

            @pl.when(z > 0)
            def _():
                send_down(n).start()

        e = i - delay

        @pl.when((e >= 0) & (e < steps))
        def _():
            s[4 * e + q] = (
                ups[e].astype(jnp.float32) + downs[e].astype(jnp.float32) - part[e].astype(jnp.float32)
            ).astype(jnp.bfloat16)
            sum_y(e).start()
            sum_core(e).start()

        f = i - delay - 1

        @pl.when((f >= 0) & (f < steps))
        def _():
            sum_y(f).wait_recv()
            sum_pass(f).start()

        h = i - delay - 2

        @pl.when(h >= 0)
        def _():
            sum_core(h).wait_recv()
            sum_pass(h).wait_recv()

            def one(r, carry):
                multiply(4 * h + r, acc, x_ref)
                return carry

            lax.fori_loop(0, 4, one, 0)

        return carry

    lax.fori_loop(0, steps + delay + 2, step, 0)

    def turn(t, carry):
        first = acc[:, at(t)]
        mid[:, at(t)] = (2.0315 * first).astype(jnp.bfloat16)
        acc[:, at(t)] = 3.4445 * x_ref[:, at(t)].astype(jnp.float32) - 4.775 * first
        return carry

    lax.fori_loop(0, chunks, turn, 0)

    def last(b, carry):
        multiply(b, acc, mid)
        return carry

    lax.fori_loop(0, 4 * steps, last, 0)
    scale = math.sqrt(max(rows * count, width))

    def write(t, carry):
        o_ref[:, at(t)] = (acc[:, at(t)] * scale).astype(o_ref.dtype)
        return carry

    lax.fori_loop(0, chunks, write, 0)

    def drain_x(t, carry):
        send_core(t).wait_send()
        pass_core(t).wait_send()
        return carry

    lax.fori_loop(0, chunks, drain_x, 0)

    def drain(k, carry):
        @pl.when(z < planes - 1)
        def _():
            send_up(k).wait_send()

        @pl.when(z > 0)
        def _():
            send_down(k).wait_send()

        sum_y(k).wait_send()
        sum_core(k).wait_send()
        sum_pass(k).wait_send()
        return carry

    lax.fori_loop(0, steps, drain, 0)


def body(iterate):
    rows, width = iterate.shape
    planes = lax.axis_size("row") // 4
    chunks = width // WIDE
    blocks = chunks * (chunks + 1) // 2
    steps = blocks // 4
    block = (WIDE, WIDE)
    return pl.pallas_call(
        functools.partial(kernel, planes),
        out_shape=jax.ShapeDtypeStruct((rows, width), jnp.bfloat16),
        in_specs=[pl.BlockSpec(memory_space=pltpu.VMEM)],
        out_specs=pl.BlockSpec(memory_space=pltpu.VMEM),
        scratch_shapes=[
            pltpu.VMEM((4 * rows, width), jnp.bfloat16),
            pltpu.VMEM((blocks,) + block, jnp.bfloat16),
            pltpu.VMEM((steps,) + block, jnp.bfloat16),
            pltpu.VMEM((steps,) + block, jnp.bfloat16),
            pltpu.VMEM((steps,) + block, jnp.bfloat16),
            pltpu.VMEM((rows, width), jnp.float32),
            pltpu.VMEM((rows, width), jnp.bfloat16),
        ]
        + [pltpu.SemaphoreType.DMA((chunks,))] * 6
        + [pltpu.SemaphoreType.DMA((steps,))] * 10,
        compiler_params=pltpu.CompilerParams(
            collective_id=0, has_side_effects=True, vmem_limit_bytes=62 * 1024 * 1024
        ),
        cost_estimate=pl.CostEstimate(flops=30 * 10**9, bytes_accessed=4 * rows * width, transcendentals=0),
    )(iterate)


def solution(mesh):
    spec = P(("layers", "row"), None)
    return jax.shard_map(body, mesh=mesh, in_specs=(spec,), out_specs=spec, check_vma=False)
```

time: 313 us -> 216 us (0.69)
  waiting for transfers between devices: 213 us -> 0 us
  Pallas kernels: 0 us -> 212 us
  matrix products: 84.9 us -> 0 us
  between operations: 13.4 us -> 0.01 us
    all_gather x1 -> x0, waiting for transfers between devices: 212 us -> none  [body(): whole = lax.all_gather(iterate, 'row', axis=0, tiled=True)]
    pallas_call x0 -> x1, Pallas kernels: none -> 212 us  [body(): pl.pallas_call(functools.partial(kernel, planes), out_shape=jax.ShapeDtyp...]
    dot_general x4 -> x0, matrix products: 84.9 us -> none  [the longest x1 23.1 us: body(): jnp.dot(poly, whole, preferred_element_type=jnp.float32)]
  transfers between devices with their start and end apart: 1 -> 0, of which waited for: 1 -> 0; matrix products, arithmetic and copies ran while one was open for 0% -> 0% of each run, Pallas kernels for 0% -> 0%
where the time goes in v1:
time: 216 us; the launch traced here: 215 us
  Pallas kernels  212 us (98%)
  local copies, waits for them, and re-layouts  3.53 us (2%)
    pallas_call x1, Pallas kernels, body(): pl.pallas_call(functools.partial(kernel, planes), out_shape=jax.ShapeDtyp...  212 us

profile of v1, /device:TPU:0, one launch (start us, length us, event | category | flops | bytes accessed | tf_op | source)
XLA Modules:
  0.0 215.4 jit_solution(336249227828119542)
XLA Ops:
  0.0 211.9 %shard_map.17 = bf16[320,4096]{1,0:T(8,128)(2,1)} custom-call(bf16[320,4096]{1,0:T(8,128)(2,1)} %x_ref.1), custom_call_target="tpu_custom_call" | custom-call | flops 30000001024 | bytes 5242880 | tf_op jit(solution)/shard_map/pallas_call | solution.py:246
  211.9 3.5 %copy.3 = bf16[320,4096]{1,0:T(8,128)(2,1)} copy(bf16[320,4096]{1,0:T(8,128)(2,1)} %shard_map.17) | data formatting | bytes 5242880

commit v2 on v1

v2 whole, which is shorter than its diff:
```python
import functools
import math

import jax
import jax.numpy as jnp
from jax import lax
from jax.experimental import pallas as pl
from jax.experimental.pallas import tpu as pltpu
from jax.sharding import PartitionSpec as P

WIDE = 512
SPLIT = 4
HOP = 2
LAG = 4
AHEAD = 3
MESH = pl.DeviceIdType.MESH
TN = (((0,), (0,)), ((), ()))


def kernel(planes, x_ref, o_ref, quad, s, ups, downs, acc, load, *sems):
    (xy_s, xy_r, xc_s, xc_r, xf_s, xf_r, u_s, u_r, d_s, d_r, gy_s, gy_r, gc_s, gc_r, gf_s, gf_r) = sems
    rows, width = x_ref.shape
    chunks = width // WIDE
    tall = WIDE // SPLIT
    units = ups.shape[0]
    each = 4 // SPLIT
    layer = lax.axis_index("layers")
    me = lax.axis_index("row")
    z = me // 4
    q = me % 4
    q_core = q + 1 - 2 * (q % 2)
    q_y = (q + 2) % 4
    core = me - q + q_core
    mate = me - q + q_y
    count = 4 * planes
    above = (me + 4) % count
    below = (me + count - 4) % count

    def remote(src, dst, send, recv, to):
        return pltpu.make_async_remote_copy(
            src_ref=src, dst_ref=dst, send_sem=send, recv_sem=recv, device_id=(layer, to), device_id_type=MESH
        )

    def at(t):
        return pl.ds(pl.multiple_of(t * WIDE, WIDE), WIDE)

    def of(member):
        return pl.ds(pl.multiple_of(member * rows, 16), rows)

    def send_y(t):
        piece = quad.at[of(q), at(t)]
        return remote(piece, piece, xy_s.at[t], xy_r.at[t], mate)

    def send_core(t):
        piece = quad.at[of(q), at(t)]
        return remote(piece, piece, xc_s.at[t], xc_r.at[t], core)

    def pass_core(t):
        piece = quad.at[of(q_y), at(t)]
        return remote(piece, piece, xf_s.at[t], xf_r.at[t], core)

    def send_up(k):
        return remote(ups.at[k], ups.at[k], u_s.at[k], u_r.at[k], above)

    def send_down(k):
        return remote(downs.at[k], downs.at[k], d_s.at[k], d_r.at[k], below)

    def total(u, member):
        j, t = where(4 * (u // SPLIT) + member)
        return pl.ds(pl.multiple_of(j * WIDE + (u % SPLIT) * tall, tall), tall), at(t)

    def sum_y(u):
        piece = s.at[total(u, q)]
        return remote(piece, piece, gy_s.at[u], gy_r.at[u], mate)

    def sum_core(u):
        piece = s.at[total(u, q)]
        return remote(piece, piece, gc_s.at[u], gc_r.at[u], core)

    def sum_pass(u):
        piece = s.at[total(u, q_y)]
        return remote(piece, piece, gf_s.at[u], gf_r.at[u], core)

    def where(b):
        t = 0
        for c in range(1, chunks):
            t = t + (b + 1024 - c * (c + 1) // 2) // 1024
        return b - t * (t + 1) // 2, t

    own = pltpu.make_async_copy(x_ref, quad.at[of(q)], load)
    own.start()
    barrier = pltpu.get_barrier_semaphore()
    for other in (core, mate, above, below):
        pl.semaphore_signal(barrier, inc=1, device_id=(layer, other), device_id_type=MESH)
    pl.semaphore_wait(barrier, 4)
    own.wait()

    for t in range(min(AHEAD, chunks)):
        send_y(t).start()
    for t in range(chunks):
        send_core(t).start()
    acc[...] = jnp.zeros_like(acc)

    def chunk(t):
        send_y(t).wait_recv()
        pass_core(t).start()
        send_y(t).wait_send()

        @pl.when(t + AHEAD < chunks)
        def _():
            send_y(t + AHEAD).start()

        send_core(t).wait_recv()
        pass_core(t).wait_recv()

    def multiply(b):
        j, t = where(b)
        acc[:, at(t)] += jnp.dot(quad[of(q), at(j)], s[at(j), at(t)], preferred_element_type=jnp.float32)

        @pl.when(j < t)
        def _():
            s[at(t), at(j)] = s[at(j), at(t)].T
            acc[:, at(j)] += jnp.dot(quad[of(q), at(t)], s[at(t), at(j)], preferred_element_type=jnp.float32)

    chunk(0)
    chunk(1)
    delay = HOP * (planes - 1)

    def step(i, carry):
        k = i // SPLIT

        @pl.when((i % SPLIT == 0) & (i < units))
        def _():
            @pl.when(k + 2 < chunks)
            def _():
                chunk(k + 2)

            j, t = where(4 * k + q)
            s[at(j), at(t)] = lax.dot_general(
                quad[:, at(j)], quad[:, at(t)], TN, preferred_element_type=jnp.float32
            ).astype(jnp.bfloat16)

        u = i - HOP * z

        @pl.when((u >= 0) & (u < units))
        def _():
            @pl.when(z == 0)
            def _():
                ups[u] = s[total(u, q)]

            @pl.when(z > 0)
            def _():
                send_up(u).wait_recv()
                ups[u] = (ups[u].astype(jnp.float32) + s[total(u, q)].astype(jnp.float32)).astype(jnp.bfloat16)

            @pl.when(z < planes - 1)
            def _():
                send_up(u).start()

        n = i - HOP * (planes - 1 - z)

        @pl.when((n >= 0) & (n < units))
        def _():
            @pl.when(z == planes - 1)
            def _():
                downs[n] = s[total(n, q)]

            @pl.when(z < planes - 1)
            def _():
                send_down(n).wait_recv()
                downs[n] = (downs[n].astype(jnp.float32) + s[total(n, q)].astype(jnp.float32)).astype(jnp.bfloat16)

            @pl.when(z > 0)
            def _():
                send_down(n).start()

        e = i - delay

        @pl.when((e >= 0) & (e < units))
        def _():
            mine = s[total(e, q)].astype(jnp.float32)
            s[total(e, q)] = (ups[e].astype(jnp.float32) + downs[e].astype(jnp.float32) - mine).astype(jnp.bfloat16)
            sum_y(e).start()
            sum_core(e).start()

        f = e - LAG

        @pl.when((f >= 0) & (f < units))
        def _():
            sum_y(f).wait_recv()
            sum_pass(f).start()

        h = f - 1

        @pl.when((h >= 0) & (h < units))
        def _():
            sum_core(h).wait_recv()
            sum_pass(h).wait_recv()

        @pl.when(h >= SPLIT)
        def _():
            for r in range(each):
                multiply((h - SPLIT) * each + r)

        return carry

    lax.fori_loop(0, units + delay + LAG + 1 + SPLIT, step, 0)

    def turn(t, carry):
        quad[of(q_core), at(t)] = (2.0315 * acc[:, at(t)]).astype(jnp.bfloat16)
        return carry

    lax.fori_loop(0, chunks, turn, 0)
    scale = math.sqrt(max(rows * count, width))

    def write(t, carry):
        after = jnp.dot(quad[of(q_core), :], s[:, at(t)], preferred_element_type=jnp.float32)
        after += 3.4445 * quad[of(q), at(t)].astype(jnp.float32) - 4.775 * acc[:, at(t)]
        o_ref[:, at(t)] = (after * scale).astype(o_ref.dtype)
        return carry

    lax.fori_loop(0, chunks, write, 0)

    def drain_x(t, carry):
        send_core(t).wait_send()
        pass_core(t).wait_send()
        return carry

    lax.fori_loop(0, chunks, drain_x, 0)

    def drain(k, carry):
        @pl.when(z < planes - 1)
        def _():
            send_up(k).wait_send()

        @pl.when(z > 0)
        def _():
            send_down(k).wait_send()

        sum_y(k).wait_send()
        sum_core(k).wait_send()
        sum_pass(k).wait_send()
        return carry

    lax.fori_loop(0, units, drain, 0)


def body(iterate):
    rows, width = iterate.shape
    planes = lax.axis_size("row") // 4
    chunks = width // WIDE
    blocks = chunks * (chunks + 1) // 2
    units = blocks // 4 * SPLIT
    piece = (units, WIDE // SPLIT, WIDE)
    return pl.pallas_call(
        functools.partial(kernel, planes),
        out_shape=jax.ShapeDtypeStruct((rows, width), jnp.bfloat16),
        in_specs=[pl.BlockSpec(memory_space=pl.ANY)],
        out_specs=pl.BlockSpec(memory_space=pltpu.VMEM),
        scratch_shapes=[
            pltpu.VMEM((4 * rows, width), jnp.bfloat16),
            pltpu.VMEM((width, width), jnp.bfloat16),
            pltpu.VMEM(piece, jnp.bfloat16),
            pltpu.VMEM(piece, jnp.bfloat16),
            pltpu.VMEM((rows, width), jnp.float32),
            pltpu.SemaphoreType.DMA,
        ]
        + [pltpu.SemaphoreType.DMA((chunks,))] * 6
        + [pltpu.SemaphoreType.DMA((units,))] * 10,
        compiler_params=pltpu.CompilerParams(
            collective_id=0, has_side_effects=True, vmem_limit_bytes=62 * 1024 * 1024
        ),
        cost_estimate=pl.CostEstimate(flops=30 * 10**9, bytes_accessed=4 * rows * width, transcendentals=0),
    )(iterate)


def solution(mesh):
    spec = P(("layers", "row"), None)
    return jax.shard_map(body, mesh=mesh, in_specs=(spec,), out_specs=spec, check_vma=False)
```

time: 216 us -> 191 us (0.88)
  Pallas kernels: 212 us -> 187 us
    pallas_call x1, Pallas kernels: 212 us -> 187 us  [body(): pl.pallas_call(functools.partial(kernel, planes), out_shape=jax.ShapeDtyp...]
where the time goes in v2:
time: 191 us
  Pallas kernels  187 us (98%)
  local copies, waits for them, and re-layouts  3.53 us (2%)
    pallas_call x1, Pallas kernels, body(): pl.pallas_call(functools.partial(kernel, planes), out_shape=jax.ShapeDtyp...  187 us

profile of v2, /device:TPU:0, one launch (start us, length us, event | category | flops | bytes accessed | tf_op | source)
XLA Modules:
  0.0 190.8 jit_solution(5611631481283473274)
XLA Ops:
  0.0 187.3 %shard_map.17 = bf16[320,4096]{1,0:T(8,128)(2,1)} custom-call(bf16[320,4096]{1,0:T(8,128)(2,1)} %x_ref.1), custom_call_target="tpu_custom_call" | custom-call | flops 30000001024 | bytes 5242880 | tf_op jit(solution)/shard_map/pallas_call | solution.py:255
  187.3 3.5 %copy.3 = bf16[320,4096]{1,0:T(8,128)(2,1)} copy(bf16[320,4096]{1,0:T(8,128)(2,1)} %shard_map.17) | data formatting | bytes 5242880

commit v3 on v2

--- a/solution.py
+++ b/solution.py
@@ -59,27 +59,56 @@
         piece = quad.at[of(q_y), at(t)]
         return remote(piece, piece, xf_s.at[t], xf_r.at[t], core)
 
-    def send_up(k):
-        return remote(ups.at[k], ups.at[k], u_s.at[k], u_r.at[k], above)
-
-    def send_down(k):
-        return remote(downs.at[k], downs.at[k], d_s.at[k], d_r.at[k], below)
-
-    def total(u, member):
+    def send_up(k, skip):
+        piece = ups.at[k, :, pl.ds(skip, WIDE - skip)]
+        return remote(piece, piece, u_s.at[k], u_r.at[k], above)
+
+    def send_down(k, skip):
+        piece = downs.at[k, :, pl.ds(skip, WIDE - skip)]
+        return remote(piece, piece, d_s.at[k], d_r.at[k], below)
+
+    def total(u, member, skip=0):
         j, t = where(4 * (u // SPLIT) + member)
-        return pl.ds(pl.multiple_of(j * WIDE + (u % SPLIT) * tall, tall), tall), at(t)
-
-    def sum_y(u):
-        piece = s.at[total(u, q)]
+        return pl.ds(pl.multiple_of(j * WIDE + (u % SPLIT) * tall, tall), tall), pl.ds(pl.multiple_of(t * WIDE + skip, 128), WIDE - skip)
+
+    def sum_y(u, skip):
+        piece = s.at[total(u, q, skip)]
         return remote(piece, piece, gy_s.at[u], gy_r.at[u], mate)
 
-    def sum_core(u):
-        piece = s.at[total(u, q)]
+    def sum_core(u, skip):
+        piece = s.at[total(u, q, skip)]
         return remote(piece, piece, gc_s.at[u], gc_r.at[u], core)
 
-    def sum_pass(u):
-        piece = s.at[total(u, q_y)]
+    def sum_pass(u, skip):
+        piece = s.at[total(u, q_y, skip)]
         return remote(piece, piece, gf_s.at[u], gf_r.at[u], core)
+
+    def sum_y_in(u, skip):
+        piece = s.at[total(u, q_y, skip)]
+        return remote(piece, piece, gy_s.at[u], gy_r.at[u], mate)
+
+    def sum_core_in(u, skip):
+        piece = s.at[total(u, q_core, skip)]
+        return remote(piece, piece, gc_s.at[u], gc_r.at[u], core)
+
+    def sum_pass_in(u, skip):
+        piece = s.at[total(u, 3 - q, skip)]
+        return remote(piece, piece, gf_s.at[u], gf_r.at[u], core)
+
+    def only(u, member, act):
+        j, t = where(4 * (u // SPLIT) + member)
+        part = u % SPLIT
+        cut = (j == t) & (part > 0)
+
+        @pl.when(jnp.logical_not(cut))
+        def _():
+            act(0)
+
+        for p in range(1, SPLIT):
+
+            @pl.when((j == t) & (part == p))
+            def _():
+                act(p * tall)
 
     def where(b):
         t = 0
@@ -115,6 +144,14 @@
 
     def multiply(b):
         j, t = where(b)
+
+        @pl.when(j == t)
+        def _():
+            for p in range(1, SPLIT):
+                low = pl.ds(pl.multiple_of(j * WIDE + p * tall, tall), tall)
+                high = pl.ds(pl.multiple_of(j * WIDE, WIDE), p * tall)
+                s[low, high] = s[high, low].T
+
         acc[:, at(t)] += jnp.dot(quad[of(q), at(j)], s[at(j), at(t)], preferred_element_type=jnp.float32)
 
         @pl.when(j < t)
@@ -150,12 +187,12 @@
 
             @pl.when(z > 0)
             def _():
-                send_up(u).wait_recv()
+                only(u, q, lambda skip: send_up(u, skip).wait_recv())
                 ups[u] = (ups[u].astype(jnp.float32) + s[total(u, q)].astype(jnp.float32)).astype(jnp.bfloat16)
 
             @pl.when(z < planes - 1)
             def _():
-                send_up(u).start()
+                only(u, q, lambda skip: send_up(u, skip).start())
 
         n = i - HOP * (planes - 1 - z)
 
@@ -167,12 +204,12 @@
 
             @pl.when(z < planes - 1)
             def _():
-                send_down(n).wait_recv()
+                only(n, q, lambda skip: send_down(n, skip).wait_recv())
                 downs[n] = (downs[n].astype(jnp.float32) + s[total(n, q)].astype(jnp.float32)).astype(jnp.bfloat16)
 
             @pl.when(z > 0)
             def _():
-                send_down(n).start()
+                only(n, q, lambda skip: send_down(n, skip).start())
 
         e = i - delay
 
@@ -180,22 +217,26 @@
         def _():
             mine = s[total(e, q)].astype(jnp.float32)
             s[total(e, q)] = (ups[e].astype(jnp.float32) + downs[e].astype(jnp.float32) - mine).astype(jnp.bfloat16)
-            sum_y(e).start()
-            sum_core(e).start()
+
+            def share(skip):
+                sum_y(e, skip).start()
+                sum_core(e, skip).start()
+
+            only(e, q, share)
 
         f = e - LAG
 
         @pl.when((f >= 0) & (f < units))
         def _():
-            sum_y(f).wait_recv()
-            sum_pass(f).start()
+            only(f, q_y, lambda skip: sum_y_in(f, skip).wait_recv())
+            only(f, q_y, lambda skip: sum_pass(f, skip).start())
 
         h = f - 1
 
         @pl.when((h >= 0) & (h < units))
         def _():
-            sum_core(h).wait_recv()
-            sum_pass(h).wait_recv()
+            only(h, q_core, lambda skip: sum_core_in(h, skip).wait_recv())
+            only(h, 3 - q, lambda skip: sum_pass_in(h, skip).wait_recv())
 
         @pl.when(h >= SPLIT)
         def _():
@@ -231,15 +272,15 @@
     def drain(k, carry):
         @pl.when(z < planes - 1)
         def _():
-            send_up(k).wait_send()
+            only(k, q, lambda skip: send_up(k, skip).wait_send())
 
         @pl.when(z > 0)
         def _():
-            send_down(k).wait_send()
-
-        sum_y(k).wait_send()
-        sum_core(k).wait_send()
-        sum_pass(k).wait_send()
+            only(k, q, lambda skip: send_down(k, skip).wait_send())
+
+        only(k, q, lambda skip: sum_y(k, skip).wait_send())
+        only(k, q, lambda skip: sum_core(k, skip).wait_send())
+        only(k, q_y, lambda skip: sum_pass(k, skip).wait_send())
         return carry
 
     lax.fori_loop(0, units, drain, 0)

time: 191 us -> 189 us (0.990)
  Pallas kernels: 187 us -> 185 us
where the time goes in v3:
time: 189 us
  Pallas kernels  185 us (98%)
  local copies, waits for them, and re-layouts  3.53 us (2%)
    pallas_call x1, Pallas kernels, body(): pl.pallas_call(functools.partial(kernel, planes), out_shape=jax.ShapeDtyp...  185 us

profile of v3, /device:TPU:0, one launch (start us, length us, event | category | flops | bytes accessed | tf_op | source)
XLA Modules:
  0.0 189.0 jit_solution(150951488479420479)
XLA Ops:
  0.0 185.5 %shard_map.17 = bf16[320,4096]{1,0:T(8,128)(2,1)} custom-call(bf16[320,4096]{1,0:T(8,128)(2,1)} %x_ref.1), custom_call_target="tpu_custom_call" | custom-call | flops 30000001024 | bytes 5242880 | tf_op jit(solution)/shard_map/pallas_call | solution.py:296
  185.5 3.5 %copy.3 = bf16[320,4096]{1,0:T(8,128)(2,1)} copy(bf16[320,4096]{1,0:T(8,128)(2,1)} %shard_map.17) | data formatting | bytes 5242880
